TPU v7x, 32 devices: a whole 2x2x4 slice. The times are simulated.
32 devices in a mesh: lon: 8 (over y, x, core), lat: 4 (over z).
Axes of the slice: x: 2, y: 2, z: 4, core: 2. Of those that a mesh axis runs over, the one named last changes fastest.
Arguments:
- state: float32 [2, 4, 360, 512], P(None, None, 'lon', 'lat'), may hold values from -6 to 6
- courant: float32 [2, 360, 512], P(None, 'lon', 'lat'), may hold values from 1 to 2160
- band_mask: int32 [512], P('lat'), may hold values 0 or 1
Outputs:
- updated: float32 [2, 4, 360, 512], P(None, None, 'lon', 'lat')
All inputs are finite; a program needn't handle non-finite values. No bound on the sum of `band_mask` on one device may be relied on, other than what follows from the above.
Results may differ from a plain program's by a relative error of at most 0.00029.
Values sent between devices are 32-bit elements; how exact they have to be, the bound alone decides.
A program may use at most 64 MiB of HBM per device.

v0:
```python
import jax
import jax.numpy as jnp
from jax import lax
from jax.sharding import PartitionSpec as P

ITERS = 2


def padded_2(block, sides, width):
    for axis, dim in sides:
        count = lax.axis_size(axis)
        forward = [(i, i + 1) for i in range(count - 1)]
        forward.append((count - 1, 0))
        backward = [(target, source) for source, target in forward]
        low = lax.ppermute(
            lax.slice_in_dim(block, block.shape[dim] - width, None, axis=dim), axis, forward
        )
        high = lax.ppermute(lax.slice_in_dim(block, 0, width, axis=dim), axis, backward)
        block = jnp.concatenate([low, block, high], axis=dim)
    return block


def from_behind(value, axis, steps):
    count = lax.axis_size(axis)
    pairs = [(source, (source + steps) % count) for source in range(count)]
    return lax.ppermute(value, axis, pairs)


def compose(earlier, later):
    return (later[0] * earlier[0], later[0][..., None, :] * earlier[1] + later[1])


def local_level(operands):
    logs_level, weights_level = operands
    spread_log = logs_level[:, None, :] - logs_level[None, :, :]
    count = logs_level.shape[0]
    below_diag = (jnp.arange(count)[:, None] >= jnp.arange(count)[None, :])[:, :, None]
    green = jnp.where(below_diag, jnp.exp(jnp.minimum(spread_log, 0.0)), 0.0)
    return jnp.einsum("ikr,fkr->fir", green, weights_level, precision=lax.Precision.HIGHEST)


def tendency(field, turning, first_band, last_band, half_cycle):
    padded = padded_2(field, (("lon", 2), ("lat", 3)), 1)
    poles = jnp.stack((field[..., 0], field[..., -1]), 0)
    across = from_behind(poles, "lon", half_cycle)
    flips = jnp.array([-1.0, -1.0, 1.0, 1.0], jnp.float32)[None, :, None]
    north_rim = jnp.where(first_band, across[0] * flips, padded[:, :, 1:-1, 0])
    south_rim = jnp.where(last_band, across[1] * flips, padded[:, :, 1:-1, -1])
    padded = padded.at[:, :, 1:-1, 0].set(north_rim).at[:, :, 1:-1, -1].set(south_rim)
    north_rows = padded[:, :, 1:-1, :-2]
    south_rows = padded[:, :, 1:-1, 2:]
    east_cells = padded[:, :, 2:, 1:-1]
    west_cells = padded[:, :, :-2, 1:-1]
    u_wind = field[:, 0:1]
    v_wind = field[:, 1:2]
    result = 0.1 * (east_cells + west_cells - 2.0 * field) + 0.1 * (
        north_rows + south_rows - 2.0 * field
    )
    result = result - 0.25 * v_wind * (north_rows - south_rows)
    coriolis = jnp.concatenate(
        [turning * v_wind, -turning * u_wind, jnp.zeros_like(field[:, 2:])], axis=1
    )
    return result + coriolis


def local(state, courant, band_mask):
    rows = state.shape[3]
    lat_index = lax.axis_index("lat")
    lat_count = lax.axis_size("lat")
    half_cycle = lax.axis_size("lon") // 2
    total_rows = rows * lat_count
    row_ids = lat_index * rows + jnp.arange(rows, dtype=jnp.int32)
    latitude = jnp.pi / 2 - (row_ids.astype(jnp.float32) + 0.5) * jnp.pi / total_rows
    turning = 0.5 * jnp.sin(latitude)
    first_band = lat_index == 0
    last_band = lat_index == lat_count - 1
    inverse = 1.0 / (1.0 + courant)
    logs = jnp.cumsum(-jnp.log1p(1.0 / courant), axis=1)
    carried = jnp.exp(logs)
    map_gain = carried[:, -1, :]
    in_band = (band_mask == 1)[None, None, None, :]
    estimate = state
    for sweep in range(ITERS):
        middle = 0.5 * (state + estimate)
        star = state + tendency(middle, turning, first_band, last_band, half_cycle)
        partial_value = lax.map(local_level, (logs, star * inverse[:, None]))
        ends = partial_value[:, :, -1, :]
        maps_a, maps_b = (
            lax.all_gather(map_gain[None], "lon", axis=0, tiled=True),
            lax.all_gather(ends[None], "lon", axis=0, tiled=True),
        )
        run_a, run_b = lax.associative_scan(compose, (maps_a, maps_b), axis=0)
        lon_index = lax.axis_index("lon")
        prior = jnp.maximum(lon_index - 1, 0)
        at_start = lon_index == 0
        prior_a = jnp.where(
            at_start, 1.0, lax.dynamic_index_in_dim(run_a, prior, 0, keepdims=False)
        )
        prior_b = jnp.where(
            at_start, 0.0, lax.dynamic_index_in_dim(run_b, prior, 0, keepdims=False)
        )
        total_a = run_a[-1]
        total_b = run_b[-1]
        wrapped = total_b / (1.0 - total_a)[:, None, :]
        inflow = prior_b + prior_a[:, None, :] * wrapped
        solved = partial_value + carried[:, None] * inflow[:, :, None, :]
        estimate = jnp.where(in_band, solved, star)
    return estimate


def solution(mesh):
    in_specs = (P(None, None, "lon", "lat"), P(None, "lon", "lat"), P("lat"))
    out_specs = P(None, None, "lon", "lat")
    return jax.shard_map(local, mesh=mesh, in_specs=in_specs, out_specs=out_specs, check_vma=False)
```

profile of v0, /device:TPU:0, one launch (start us, length us, event | category | flops | bytes accessed | tf_op | source)
XLA Modules:
  0.0 128.2 jit_solution(9289182987580346794)
XLA Ops:
  0.0 1.0 add_multiply_fusion
  1.0 0.5 collective-permute-start
  1.5 3.0 %collective-permute-start.1 = (f32[2,4,1,128]{3,0,2,1:T(2,128)S(1)}, f32[2,4,1,128]{3,0,2,1:T(2,128)S(1)}, u32[]{:S(2)}, u32[]{:S(2)}) collective-permute-start(f32[2,4,1,128]{3,0,2,1:T(2,128)S(1)} %get-tuple-element.213), channel_id=1, source_target_pairs={{4,0},{8,4},{12,8},{16,12},{20,16},{24,20},{28,24},{0,28},{5,1},{9... | collective-permute-start | bytes 12296 | tf_op jit(solution)/shard_map/ppermute | solution.py:18
  4.5 0.3 fusion.72
  4.8 0.1 copy.394
  4.9 0.1 copy.395
  5.0 2.3 %collective-permute-start.4 = (f32[2,2,4,45]{3,2,1,0:T(4,128)S(1)}, f32[2,2,4,45]{3,2,1,0:T(4,128)S(1)}, u32[]{:S(2)}, u32[]{:S(2)}) collective-permute-start(f32[2,2,4,45]{3,2,1,0:T(4,128)S(1)} %pad_maximum_fusion.6), channel_id=1, source_target_pairs={{0,16},{4,20},{8,24},{12,28},{16,0},{20,4},{24,8},{28,12},{1,17},{... | collective-permute-start | bytes 8648 | tf_op jit(solution)/shard_map/ppermute | solution.py:26
  7.5 8.0 %all-gather.1 = f32[16,1,128]{2,1,0:T(1,128)S(1)} all-gather(f32[2,1,128]{2,1,0:T(1,128)S(1)} %slice.463), channel_id=3, replica_groups=mesh['lon'=8,'lat'=4] {'lon'}, dimensions={0}, use_global_device_ids=true | all-gather | bytes 9216 | tf_op jit(solution)/shard_map/all_gather | solution.py:89
  16.0 0.1 copy.401
  16.3 0.3 fusion.69
  16.6 1.6 %collective-permute-start.2 = (f32[2,4,47,1]{3,0,2,1:T(2,128)S(1)}, f32[2,4,47,1]{3,0,2,1:T(2,128)S(1)}, u32[]{:S(2)}, u32[]{:S(2)}) collective-permute-start(f32[2,4,47,1]{3,0,2,1:T(2,128)S(1)} %get-tuple-element.201), channel_id=1, source_target_pairs={{0,1},{1,2},{2,3},{3,0},{4,5},{5,6},{6,7},{7,4},{8,9},{9,10},{10,1... | collective-permute-start | bytes 4520 | tf_op jit(solution)/shard_map/ppermute | solution.py:15
  18.2 2.2 %collective-permute-start.3 = (f32[2,4,47,1]{3,0,2,1:T(2,128)S(1)}, f32[2,4,47,1]{3,0,2,1:T(2,128)S(1)}, u32[]{:S(2)}, u32[]{:S(2)}) collective-permute-start(f32[2,4,47,1]{3,0,2,1:T(2,128)S(1)} %get-tuple-element.202), channel_id=1, source_target_pairs={{1,0},{2,1},{3,2},{0,3},{5,4},{6,5},{7,6},{4,7},{9,8},{10,9},{11,1... | collective-permute-start | bytes 4520 | tf_op jit(solution)/shard_map/ppermute | solution.py:18
  20.5 0.2 copy.396
  20.6 0.2 copy.397
  20.8 5.3 %collective-permute-done.2 = f32[2,4,47,1]{3,0,2,1:T(2,128)S(1)} collective-permute-done((f32[2,4,47,1]{3,0,2,1:T(2,128)S(1)}, f32[2,4,47,1]{3,0,2,1:T(2,128)S(1)}, u32[]{:S(2)}, u32[]{:S(2)}) %collective-permute-start.2) | collective-permute-done | bytes 1536 | tf_op jit(solution)/shard_map/ppermute | solution.py:15
  26.1 3.0 %collective-permute-done.3 = f32[2,4,47,1]{3,0,2,1:T(2,128)S(1)} collective-permute-done((f32[2,4,47,1]{3,0,2,1:T(2,128)S(1)}, f32[2,4,47,1]{3,0,2,1:T(2,128)S(1)}, u32[]{:S(2)}, u32[]{:S(2)}) %collective-permute-start.3) | collective-permute-done | bytes 1536 | tf_op jit(solution)/shard_map/ppermute | solution.py:18
  29.1 0.7 pad_maximum_fusion
  29.8 0.3 slice_select_fusion.2
  30.0 2.8 %scatter.14 = f32[2,4,47,130]{3,0,2,1:T(2,128)S(1)} dynamic-update-slice(f32[2,4,47,130]{3,0,2,1:T(2,128)S(1)} %pad_maximum_fusion, f32[2,4,45,1]{3,0,2,1:T(2,128)S(1)} %get-tuple-element.250, s32[]{:T(128)} %copy.493, s32[]{:T(128)} %copy.493, s32[]{:T(128)} %constant.178.clone.1, s32[]{:T(128)} %copy.493) | dynamic-update-slice | bytes 2884 | tf_op jit(solution)/shard_map/scatter | solution.py:49
  32.9 14.9 %scatter.15 = f32[2,4,47,130]{3,0,2,1:T(2,128)S(1)} dynamic-update-slice(f32[2,4,47,130]{3,0,2,1:T(2,128)S(1)} %scatter.14, f32[2,4,45,1]{3,0,2,1:T(2,128)S(1)} %get-tuple-element.249, s32[]{:T(128)} %copy.493, s32[]{:T(128)} %copy.493, s32[]{:T(128)} %constant.178.clone.1, s32[]{:T(128)} %constant.185.clone.1) | dynamic-update-slice | bytes 2884 | tf_op jit(solution)/shard_map/scatter | solution.py:49
  47.8 0.7 broadcast_multiply_fusion.1
  48.5 11.2 %while.24 = (s32[]{:T(128)}, f32[2,4,45,128]{2,1,3,0:T(4,128)S(1)}, f32[2,4,45,128]{3,0,2,1:T(2,128)S(1)}, f32[2,45,128]{1,2,0:T(8,128)S(1)}, s32[]{:T(128)}) while((s32[]{:T(128)}, f32[2,4,45,128]{2,1,3,0:T(4,128)S(1)}, f32[2,4,45,128]{3,0,2,1:T(2,128)S(1)}, f32[2,45,128]{1,2,0:T(8,128)S(1)}, s32[]{:T(128)}) %tuple.99), condition=%wide.region_2.3_spmd, body=%wide.region_1.2_spmd.sunk | while | flops 13221227 | bytes 1078322 | solution.py:86
  48.6 0.2 copy.456
  48.8 5.3 %fusion.90 = f32[2,4,45,128]{2,1,3,0:T(4,128)S(1)} fusion(f32[2,4,45,128]{2,1,3,0:T(4,128)S(1)} %get-tuple-element.311, s32[]{:T(128)} %get-tuple-element.310, f32[45,128]{0,1:T(8,128)S(1)} %dynamic-slice_bitcast_fusion.4, pred[45,45]{1,0:T(8,128)(4,1)S(1)} %iota_compare_fusion.4, f32[1,4,45,128]{2,1,3,0:T(4,128)S(1)} %copy.456), kind=kOutput, calls=%fused_computation.10.clone.1 | convolution fusion | flops 13219200 | bytes 661508 | tf_op jit(solution)/shard_map/while/body/eval_jaxpr/ikr,fkr->fir/dot_general | solution.py:39
  54.2 0.2 copy.456
  54.4 5.3 %fusion.90 = f32[2,4,45,128]{2,1,3,0:T(4,128)S(1)} fusion(f32[2,4,45,128]{2,1,3,0:T(4,128)S(1)} %get-tuple-element.311, s32[]{:T(128)} %get-tuple-element.310, f32[45,128]{0,1:T(8,128)S(1)} %dynamic-slice_bitcast_fusion.4, pred[45,45]{1,0:T(8,128)(4,1)S(1)} %iota_compare_fusion.4, f32[1,4,45,128]{2,1,3,0:T(4,128)S(1)} %copy.456), kind=kOutput, calls=%fused_computation.10.clone.1 | convolution fusion | flops 13219200 | bytes 661508 | tf_op jit(solution)/shard_map/while/body/eval_jaxpr/ikr,fkr->fir/dot_general | solution.py:39
  59.7 0.2 copy.403
  59.9 9.2 %all-gather = f32[16,4,1,128]{3,1,2,0:T(4,128)S(1)} all-gather(f32[2,4,1,128]{3,1,2,0:T(4,128)S(1)} %slice.461), channel_id=2, replica_groups=mesh['lon'=8,'lat'=4] {'lon'}, dimensions={0}, use_global_device_ids=true | all-gather | bytes 36864 | tf_op jit(solution)/shard_map/all_gather | solution.py:90
  69.2 0.2 copy.409
  69.6 0.1 pad.84
  69.7 0.1 pad.223
  69.9 0.1 pad.83
  70.0 0.2 broadcast_multiply_fusion.2
  70.2 0.3 fusion.70
  70.5 0.1 copy.411
  70.7 0.1 copy.412
  70.8 0.4 collective-permute-start.5
  71.2 2.3 %collective-permute-start.6 = (f32[2,4,1,128]{3,0,2,1:T(2,128)S(1)}, f32[2,4,1,128]{3,0,2,1:T(2,128)S(1)}, u32[]{:S(2)}, u32[]{:S(2)}) collective-permute-start(f32[2,4,1,128]{3,0,2,1:T(2,128)S(1)} %get-tuple-element.206), channel_id=1, source_target_pairs={{4,0},{8,4},{12,8},{16,12},{20,16},{24,20},{28,24},{0,28},{5,1},{9... | collective-permute-start | bytes 12296 | tf_op jit(solution)/shard_map/ppermute | solution.py:18
  73.5 0.6 collective-permute-start.9
  74.1 0.7 collective-permute-done.5
  74.9 0.3 fusion.68
  75.2 1.2 collective-permute-start.7
  76.3 2.7 %collective-permute-start.8 = (f32[2,4,47,1]{3,0,2,1:T(2,128)S(1)}, f32[2,4,47,1]{3,0,2,1:T(2,128)S(1)}, u32[]{:S(2)}, u32[]{:S(2)}) collective-permute-start(f32[2,4,47,1]{3,0,2,1:T(2,128)S(1)} %get-tuple-element.200), channel_id=1, source_target_pairs={{1,0},{2,1},{3,2},{0,3},{5,4},{6,5},{7,6},{4,7},{9,8},{10,9},{11,1... | collective-permute-start | bytes 4520 | tf_op jit(solution)/shard_map/ppermute | solution.py:18
  79.0 0.2 copy.413
  79.2 0.2 copy.414
  79.4 5.3 %collective-permute-done.7 = f32[2,4,47,1]{3,0,2,1:T(2,128)S(1)} collective-permute-done((f32[2,4,47,1]{3,0,2,1:T(2,128)S(1)}, f32[2,4,47,1]{3,0,2,1:T(2,128)S(1)}, u32[]{:S(2)}, u32[]{:S(2)}) %collective-permute-start.7) | collective-permute-done | bytes 1536 | tf_op jit(solution)/shard_map/ppermute | solution.py:15
  84.7 2.2 %collective-permute-done.8 = f32[2,4,47,1]{3,0,2,1:T(2,128)S(1)} collective-permute-done((f32[2,4,47,1]{3,0,2,1:T(2,128)S(1)}, f32[2,4,47,1]{3,0,2,1:T(2,128)S(1)}, u32[]{:S(2)}, u32[]{:S(2)}) %collective-permute-start.8) | collective-permute-done | bytes 1536 | tf_op jit(solution)/shard_map/ppermute | solution.py:18
  87.0 0.7 pad_maximum_fusion.1
  87.6 0.3 slice_select_fusion
  87.9 2.8 %scatter.16 = f32[2,4,47,130]{3,0,2,1:T(2,128)S(1)} dynamic-update-slice(f32[2,4,47,130]{3,0,2,1:T(2,128)S(1)} %pad_maximum_fusion.1, f32[2,4,45,1]{3,0,2,1:T(2,128)S(1)} %get-tuple-element.248, s32[]{:T(128)} %copy.493, s32[]{:T(128)} %copy.493, s32[]{:T(128)} %constant.178.clone.1, s32[]{:T(128)} %copy.493) | dynamic-update-slice | bytes 2884 | tf_op jit(solution)/shard_map/scatter | solution.py:49
  90.7 14.9 %scatter.19 = f32[2,4,47,130]{3,0,2,1:T(2,128)S(1)} dynamic-update-slice(f32[2,4,47,130]{3,0,2,1:T(2,128)S(1)} %scatter.16, f32[2,4,45,1]{3,0,2,1:T(2,128)S(1)} %get-tuple-element.247, s32[]{:T(128)} %copy.493, s32[]{:T(128)} %copy.493, s32[]{:T(128)} %constant.178.clone.1, s32[]{:T(128)} %constant.185.clone.1) | dynamic-update-slice | bytes 2884 | tf_op jit(solution)/shard_map/scatter | solution.py:49
  105.6 0.7 broadcast_multiply_fusion
  106.4 11.2 %while.25 = (s32[]{:T(128)}, f32[2,4,45,128]{2,1,3,0:T(4,128)S(1)}, f32[2,4,45,128]{3,0,2,1:T(2,128)S(1)}, f32[2,45,128]{1,2,0:T(8,128)S(1)}, s32[]{:T(128)}) while((s32[]{:T(128)}, f32[2,4,45,128]{2,1,3,0:T(4,128)S(1)}, f32[2,4,45,128]{3,0,2,1:T(2,128)S(1)}, f32[2,45,128]{1,2,0:T(8,128)S(1)}, s32[]{:T(128)}) %tuple.105), condition=%wide.region_4.5_spmd, body=%wide.region_3.4_spmd.sunk | while | flops 13221227 | bytes 1078322 | solution.py:86
  106.5 0.2 copy.457
  106.7 5.3 %fusion.93 = f32[2,4,45,128]{2,1,3,0:T(4,128)S(1)} fusion(f32[2,4,45,128]{2,1,3,0:T(4,128)S(1)} %get-tuple-element.326, s32[]{:T(128)} %get-tuple-element.325, f32[45,128]{0,1:T(8,128)S(1)} %dynamic-slice_bitcast_fusion.5, pred[45,45]{1,0:T(8,128)(4,1)S(1)} %iota_compare_fusion.5, f32[1,4,45,128]{2,1,3,0:T(4,128)S(1)} %copy.457), kind=kOutput, calls=%fused_computation.26.clone.1 | convolution fusion | flops 13219200 | bytes 661508 | tf_op jit(solution)/shard_map/while/body/eval_jaxpr/ikr,fkr->fir/dot_general | solution.py:39
  112.1 0.2 copy.457
  112.3 5.3 %fusion.93 = f32[2,4,45,128]{2,1,3,0:T(4,128)S(1)} fusion(f32[2,4,45,128]{2,1,3,0:T(4,128)S(1)} %get-tuple-element.326, s32[]{:T(128)} %get-tuple-element.325, f32[45,128]{0,1:T(8,128)S(1)} %dynamic-slice_bitcast_fusion.5, pred[45,45]{1,0:T(8,128)(4,1)S(1)} %iota_compare_fusion.5, f32[1,4,45,128]{2,1,3,0:T(4,128)S(1)} %copy.457), kind=kOutput, calls=%fused_computation.26.clone.1 | convolution fusion | flops 13219200 | bytes 661508 | tf_op jit(solution)/shard_map/while/body/eval_jaxpr/ikr,fkr->fir/dot_general | solution.py:39
  117.6 0.2 copy.418
  117.8 8.7 %all-gather.2 = f32[16,4,1,128]{3,1,2,0:T(4,128)S(1)} all-gather(f32[2,4,1,128]{3,1,2,0:T(4,128)S(1)} %slice.497), channel_id=4, replica_groups=mesh['lon'=8,'lat'=4] {'lon'}, dimensions={0}, use_global_device_ids=true | all-gather | bytes 36864 | tf_op jit(solution)/shard_map/all_gather | solution.py:90
  126.6 0.2 copy.424
  127.0 0.1 pad.96
  127.1 0.1 pad.227
  127.4 0.1 add_select_fusion
  127.5 0.7 copy.425
  (100 shorter events, 2.1 us)
Async XLA Ops:
  1.0 15.2 %collective-permute-start = (f32[2,4,1,128]{3,0,2,1:T(2,128)S(1)}, f32[2,4,1,128]{3,0,2,1:T(2,128)S(1)}, u32[]{:S(2)}, u32[]{:S(2)}) collective-permute-start(f32[2,4,1,128]{3,0,2,1:T(2,128)S(1)} %get-tuple-element.212), channel_id=1, source_target_pairs={{0,4},{4,8},{8,12},{12,16},{16,20},{20,24},{24,28},{28,0},{1,5},{5... | collective-permute-start | bytes 12296 | tf_op jit(solution)/shard_map/ppermute | solution.py:15
  1.5 5.8 %copy-start.1 = (f32[2,45,128]{2,0,1:T(2,128)S(1)}, f32[2,45,128]{2,0,1:T(2,128)}, u32[]{:S(2)}) copy-start(f32[2,45,128]{2,0,1:T(2,128)} %param.18) | copy-start | bytes 138244
  1.5 14.7 %collective-permute-start.1 = (f32[2,4,1,128]{3,0,2,1:T(2,128)S(1)}, f32[2,4,1,128]{3,0,2,1:T(2,128)S(1)}, u32[]{:S(2)}, u32[]{:S(2)}) collective-permute-start(f32[2,4,1,128]{3,0,2,1:T(2,128)S(1)} %get-tuple-element.213), channel_id=1, source_target_pairs={{4,0},{8,4},{12,8},{16,12},{20,16},{24,20},{28,24},{0,28},{5,1},{9... | collective-permute-start | bytes 12296 | tf_op jit(solution)/shard_map/ppermute | solution.py:18
  4.9 11.1 %copy-start.3 = (s32[128]{0:T(128)S(1)}, s32[128]{0:T(128)}, u32[]{:S(2)}) copy-start(s32[128]{0:T(128)} %param.19) | copy-start | bytes 1540
  5.0 15.4 %collective-permute-start.4 = (f32[2,2,4,45]{3,2,1,0:T(4,128)S(1)}, f32[2,2,4,45]{3,2,1,0:T(4,128)S(1)}, u32[]{:S(2)}, u32[]{:S(2)}) collective-permute-start(f32[2,2,4,45]{3,2,1,0:T(4,128)S(1)} %pad_maximum_fusion.6), channel_id=1, source_target_pairs={{0,16},{4,20},{8,24},{12,28},{16,0},{20,4},{24,8},{28,12},{1,17},{... | collective-permute-start | bytes 8648 | tf_op jit(solution)/shard_map/ppermute | solution.py:26
  16.6 9.5 %collective-permute-start.2 = (f32[2,4,47,1]{3,0,2,1:T(2,128)S(1)}, f32[2,4,47,1]{3,0,2,1:T(2,128)S(1)}, u32[]{:S(2)}, u32[]{:S(2)}) collective-permute-start(f32[2,4,47,1]{3,0,2,1:T(2,128)S(1)} %get-tuple-element.201), channel_id=1, source_target_pairs={{0,1},{1,2},{2,3},{3,0},{4,5},{5,6},{6,7},{7,4},{8,9},{9,10},{10,1... | collective-permute-start | bytes 4520 | tf_op jit(solution)/shard_map/ppermute | solution.py:15
  18.2 10.9 %collective-permute-start.3 = (f32[2,4,47,1]{3,0,2,1:T(2,128)S(1)}, f32[2,4,47,1]{3,0,2,1:T(2,128)S(1)}, u32[]{:S(2)}, u32[]{:S(2)}) collective-permute-start(f32[2,4,47,1]{3,0,2,1:T(2,128)S(1)} %get-tuple-element.202), channel_id=1, source_target_pairs={{1,0},{2,1},{3,2},{0,3},{5,4},{6,5},{7,6},{4,7},{9,8},{10,9},{11,1... | collective-permute-start | bytes 4520 | tf_op jit(solution)/shard_map/ppermute | solution.py:18
  20.8 9.0 %copy-start.2 = (f32[4]{0:T(128)S(1)}, f32[4]{0:T(128)}, u32[]{:S(2)}) copy-start(f32[4]{0:T(128)} %constant.194.clone) | copy-start | bytes 52
  30.0 17.8 %copy-start = (f32[2,4,45,128]{3,1,2,0:T(4,128)S(1)}, f32[2,4,45,128]{3,1,2,0:T(4,128)}, u32[]{:S(2)}) copy-start(f32[2,4,45,128]{3,1,2,0:T(4,128)} %param.17) | copy-start | bytes 552964
  70.8 4.0 %collective-permute-start.5 = (f32[2,4,1,128]{3,0,2,1:T(2,128)S(1)}, f32[2,4,1,128]{3,0,2,1:T(2,128)S(1)}, u32[]{:S(2)}, u32[]{:S(2)}) collective-permute-start(f32[2,4,1,128]{3,0,2,1:T(2,128)S(1)} %get-tuple-element.205), channel_id=1, source_target_pairs={{0,4},{4,8},{8,12},{12,16},{16,20},{20,24},{24,28},{28,0},{1,5},{5... | collective-permute-start | bytes 12296 | tf_op jit(solution)/shard_map/ppermute | solution.py:15
  71.2 3.7 %collective-permute-start.6 = (f32[2,4,1,128]{3,0,2,1:T(2,128)S(1)}, f32[2,4,1,128]{3,0,2,1:T(2,128)S(1)}, u32[]{:S(2)}, u32[]{:S(2)}) collective-permute-start(f32[2,4,1,128]{3,0,2,1:T(2,128)S(1)} %get-tuple-element.206), channel_id=1, source_target_pairs={{4,0},{8,4},{12,8},{16,12},{20,16},{24,20},{28,24},{0,28},{5,1},{9... | collective-permute-start | bytes 12296 | tf_op jit(solution)/shard_map/ppermute | solution.py:18
  73.5 5.6 %collective-permute-start.9 = (f32[2,2,4,45]{3,2,1,0:T(4,128)S(1)}, f32[2,2,4,45]{3,2,1,0:T(4,128)S(1)}, u32[]{:S(2)}, u32[]{:S(2)}) collective-permute-start(f32[2,2,4,45]{3,2,1,0:T(4,128)S(1)} %pad_maximum_fusion.8), channel_id=1, source_target_pairs={{0,16},{4,20},{8,24},{12,28},{16,0},{20,4},{24,8},{28,12},{1,17},{... | collective-permute-start | bytes 8648 | tf_op jit(solution)/shard_map/ppermute | solution.py:26
  75.2 9.6 %collective-permute-start.7 = (f32[2,4,47,1]{3,0,2,1:T(2,128)S(1)}, f32[2,4,47,1]{3,0,2,1:T(2,128)S(1)}, u32[]{:S(2)}, u32[]{:S(2)}) collective-permute-start(f32[2,4,47,1]{3,0,2,1:T(2,128)S(1)} %get-tuple-element.199), channel_id=1, source_target_pairs={{0,1},{1,2},{2,3},{3,0},{4,5},{5,6},{6,7},{7,4},{8,9},{9,10},{10,1... | collective-permute-start | bytes 4520 | tf_op jit(solution)/shard_map/ppermute | solution.py:15
  76.3 10.6 %collective-permute-start.8 = (f32[2,4,47,1]{3,0,2,1:T(2,128)S(1)}, f32[2,4,47,1]{3,0,2,1:T(2,128)S(1)}, u32[]{:S(2)}, u32[]{:S(2)}) collective-permute-start(f32[2,4,47,1]{3,0,2,1:T(2,128)S(1)} %get-tuple-element.200), channel_id=1, source_target_pairs={{1,0},{2,1},{3,2},{0,3},{5,4},{6,5},{7,6},{4,7},{9,8},{10,9},{11,1... | collective-permute-start | bytes 4520 | tf_op jit(solution)/shard_map/ppermute | solution.py:18
where the time goes:
time: 128 us
  local copies, waits for them, and re-layouts  41.9 us (33%)
  blocking collectives  25.9 us (20%)
  matrix products  21.1 us (16%)
  starting transfers between devices  16.7 us (13%)
  waiting for transfers between devices  16.6 us (13%)
  other arithmetic  5.27 us (4%)
    scatter x4, local copies, waits for them, and re-layouts, tendency(): padded.at[:, :, 1:-1, 0].set(north_rim).at[:, :, 1:-1, -1].set(south_rim)  35.5 us
    dot_general x4, matrix products, local_level(): jnp.einsum('ikr,fkr->fir', green, weights_level, precision=lax.Precision....  21.1 us
    all_gather x2, blocking collectives, local(): lax.all_gather(ends[None], 'lon', axis=0, tiled=True)  17.9 us
    ppermute x4, waiting for transfers between devices, padded_2(): lax.ppermute(lax.slice_in_dim(block, block.shape[dim] - width, None, axis...  11.3 us
    ppermute x4, starting transfers between devices, padded_2(): lax.ppermute(lax.slice_in_dim(block, 0, width, axis=dim), axis, backward)  10.2 us
    all_gather x1, blocking collectives, local(): lax.all_gather(map_gain[None], 'lon', axis=0, tiled=True)  7.97 us
    ppermute x4, waiting for transfers between devices, padded_2(): lax.ppermute(lax.slice_in_dim(block, 0, width, axis=dim), axis, backward)  5.28 us
    ppermute x4, starting transfers between devices, padded_2(): lax.ppermute(lax.slice_in_dim(block, block.shape[dim] - width, None, axis...  3.67 us
  transfers between devices with their start and end apart: 10, of which 5 were waited for; matrix products, arithmetic and copies ran while one was open for 2% of the time, Pallas kernels for 0%

commit v1 on v0

v1 whole, which is shorter than its diff:
```python
import functools

import jax
import jax.numpy as jnp
from jax import lax
from jax.experimental import pallas as pl
from jax.experimental.pallas import tpu as pltpu
from jax.sharding import PartitionSpec as P

ITERS = 2
MESH = pl.DeviceIdType.MESH


def kernel(n, m, x_ref, c_ref, mask_ref, out_ref, X, inv8, carried, part, mid,
           lonh, lats, lath, gains, ends, own,
           lon_send, lon_recv, lat_send, lat_recv, all_send, all_recv):
    levels, comps, L, R = x_ref.shape
    S = levels * comps
    lon = lax.axis_index("lon")
    lat = lax.axis_index("lat")
    east = lax.rem(lon + 1, n)
    west = lax.rem(lon + n - 1, n)
    across = lax.rem(lon + n // 2, n)
    first = lat == 0
    last = lat == m - 1
    north = (jnp.where(first, across, lon), jnp.where(first, lat, lat - 1))
    south = (jnp.where(last, across, lon), jnp.where(last, lat, lat + 1))
    north_slot = jnp.where(first, 0, 1)
    south_slot = jnp.where(last, 1, 0)

    barrier = pltpu.get_barrier_semaphore()

    def greet(k, _):
        pl.semaphore_signal(barrier, inc=1, device_id=(lax.rem(lon + k, n), lat), device_id_type=MESH)
        return 0

    lax.fori_loop(1, n, greet, 0)
    pl.semaphore_signal(barrier, inc=1, device_id=north, device_id_type=MESH)
    pl.semaphore_signal(barrier, inc=1, device_id=south, device_id_type=MESH)

    for g in range(0, L, 8):
        w = min(8, L - g)
        block = x_ref[:, :, g:g + w, :].reshape(S, w, R)
        X[g:g + w] = jnp.swapaxes(block, 0, 1)

    sub = lax.broadcasted_iota(jnp.int32, (S, R), 0)
    lane = lax.broadcasted_iota(jnp.int32, (S, R), 1)
    comp = sub % comps
    lower = sub < comps

    def by_level(rows):
        return jnp.where(lower, jnp.broadcast_to(rows[0], (S, R)), jnp.broadcast_to(rows[1], (S, R)))

    row_ids = (lat * R + lane).astype(jnp.float32)
    turning = 0.5 * jnp.sin(jnp.pi / 2 - (row_ids + 0.5) * (jnp.pi / (R * m)))
    turn_u = jnp.where(comp == 0, turning, 0.0)
    turn_v = jnp.where(comp == 1, -turning, 0.0)
    flips = jnp.where(comp < 2, -1.0, 1.0)
    flip_n = jnp.where(first, flips, 1.0)
    flip_s = jnp.where(last, flips, 1.0)

    def pack(src, it):
        rim_n = jnp.zeros((S, R), jnp.float32)
        rim_s = jnp.zeros((S, R), jnp.float32)
        for i in range(L):
            value = src[i]
            rim_n = jnp.where(lane == i, value if i == 0 else pltpu.roll(value, i, 1), rim_n)
            rim_s = jnp.where(lane == i, pltpu.roll(value, i + 1, 1), rim_s)
        lats[it, 0] = rim_n
        lats[it, 1] = rim_s

    def halo_copies(src, it):
        return [
            pltpu.make_async_remote_copy(
                src_ref=src.at[L - 1], dst_ref=lonh.at[it, 0], send_sem=lon_send.at[it, 0],
                recv_sem=lon_recv.at[it, 0], device_id=(east, lat), device_id_type=MESH),
            pltpu.make_async_remote_copy(
                src_ref=src.at[0], dst_ref=lonh.at[it, 1], send_sem=lon_send.at[it, 1],
                recv_sem=lon_recv.at[it, 1], device_id=(west, lat), device_id_type=MESH),
            pltpu.make_async_remote_copy(
                src_ref=lats.at[it, 0], dst_ref=lath.at[it, north_slot], send_sem=lat_send.at[it, 0],
                recv_sem=lat_recv.at[it, north_slot], device_id=north, device_id_type=MESH),
            pltpu.make_async_remote_copy(
                src_ref=lats.at[it, 1], dst_ref=lath.at[it, south_slot], send_sem=lat_send.at[it, 1],
                recv_sem=lat_recv.at[it, south_slot], device_id=south, device_id_type=MESH),
        ]

    def gather_start(src, dst, k_sem):
        def send(k, _):
            pltpu.make_async_remote_copy(
                src_ref=src, dst_ref=dst.at[k - 1], send_sem=all_send.at[k_sem],
                recv_sem=all_recv.at[k_sem], device_id=(lax.rem(lon + n - k, n), lat),
                device_id_type=MESH).start()
            return 0
        lax.fori_loop(1, n, send, 0)

    def gather_wait(dst, sem):
        pltpu.make_async_copy(dst, dst, sem).wait()

    pack(X, 0)
    pl.semaphore_wait(barrier, n + 1)
    halos = halo_copies(X, 0)
    for copy in halos:
        copy.start()

    band = mask_ref[...] == 1
    for i in range(L):
        rows = [jnp.where(band, 1.0 / (1.0 + c_ref[l, i:i + 1, :]), 1.0) for l in range(levels)]
        inv8[i] = by_level(rows)
    gain = 1.0 - inv8[0]
    carried[0] = gain
    for i in range(1, L):
        gain = gain * (1.0 - inv8[i])
        carried[i] = gain
    gather_start(carried.at[L - 1], gains, 0)

    ring = None
    for it in range(ITERS):
        src = X if it == 0 else mid
        for index in (0, 1):
            halos[index].wait_recv()
        for index in (0, 1):
            pltpu.make_async_copy(lath.at[it, index], lath.at[it, index], lat_recv.at[it, index]).wait()
        rim_n = lath[it, 0] * flip_n
        rim_s = lath[it, 1] * flip_s
        rim_w = lonh[it, 0]
        rim_e = lonh[it, 1]
        value = jnp.zeros((S, R), jnp.float32)
        for i in range(L):
            x = src[i]
            e = src[i + 1] if i + 1 < L else rim_e
            w = src[i - 1] if i > 0 else rim_w
            no = jnp.where(lane == 0, rim_n if i == 0 else pltpu.roll(rim_n, R - i, 1), pltpu.roll(x, 1, 1))
            so = jnp.where(lane == R - 1, pltpu.roll(rim_s, R - 1 - i, 1), pltpu.roll(x, R - 1, 1))
            u = by_level([src[i, l * comps:l * comps + 1, :] for l in range(levels)])
            v = by_level([src[i, l * comps + 1:l * comps + 2, :] for l in range(levels)])
            star = X[i] + (0.1 * (e + w + no + so) - 0.4 * x) - (0.25 * v) * (no - so) + (turn_u * v + turn_v * u)
            inv = inv8[i]
            value = (1.0 - inv) * value + star * inv
            part[i] = value
        own[it] = value
        gather_start(own.at[it], ends.at[it], 1 + it)
        if it == 0:
            gather_wait(gains, all_recv.at[0])
            total = carried[L - 1]
            if n <= 16:
                for k in range(n - 1):
                    total = total * gains[k]
            else:
                total = lax.fori_loop(0, n - 1, lambda k, t: t * gains[k], total)
            ring = 1.0 / (1.0 - total)
        gather_wait(ends.at[it], all_recv.at[1 + it])
        run = own[it]
        if n <= 16:
            for k in range(n - 1):
                run = run * gains[k] + ends[it, k]
        else:
            run = lax.fori_loop(0, n - 1, lambda k, r: r * gains[k] + ends[it, k], run)
        inflow = run * ring
        if it + 1 < ITERS:
            for i in range(L):
                mid[i] = 0.5 * (X[i] + (part[i] + carried[i] * inflow))
            pack(mid, it + 1)
            for copy in halos:
                copy.wait_send()
            halos = halo_copies(mid, it + 1)
            for copy in halos:
                copy.start()
        else:
            for i in range(L):
                out_ref[i] = part[i] + carried[i] * inflow
    for copy in halos:
        copy.wait_send()
    for k in range(3):
        gather_wait(gains, all_send.at[k])


def local(n, m, state, courant, band_mask):
    levels, comps, L, R = state.shape
    S = levels * comps
    f32 = jnp.float32
    cell = (L, S, R)
    out = pl.pallas_call(
        functools.partial(kernel, n, m),
        out_shape=jax.ShapeDtypeStruct(cell, f32),
        in_specs=[pl.BlockSpec(memory_space=pltpu.VMEM)] * 3,
        out_specs=pl.BlockSpec(memory_space=pltpu.VMEM),
        scratch_shapes=[
            pltpu.VMEM(cell, f32),
            pltpu.VMEM(cell, f32),
            pltpu.VMEM(cell, f32),
            pltpu.VMEM(cell, f32),
            pltpu.VMEM(cell, f32),
            pltpu.VMEM((ITERS, 2, S, R), f32),
            pltpu.VMEM((ITERS, 2, S, R), f32),
            pltpu.VMEM((ITERS, 2, S, R), f32),
            pltpu.VMEM((n - 1, S, R), f32),
            pltpu.VMEM((ITERS, n - 1, S, R), f32),
            pltpu.VMEM((ITERS, S, R), f32),
            pltpu.SemaphoreType.DMA((ITERS, 2)),
            pltpu.SemaphoreType.DMA((ITERS, 2)),
            pltpu.SemaphoreType.DMA((ITERS, 2)),
            pltpu.SemaphoreType.DMA((ITERS, 2)),
            pltpu.SemaphoreType.DMA((3,)),
            pltpu.SemaphoreType.DMA((3,)),
        ],
        compiler_params=pltpu.CompilerParams(
            collective_id=0, has_side_effects=True, vmem_limit_bytes=16 * 2**20),
    )(state, courant, band_mask.reshape(1, R))
    return out.transpose(1, 0, 2).reshape(state.shape)


def solution(mesh):
    n, m = mesh.shape["lon"], mesh.shape["lat"]
    in_specs = (P(None, None, "lon", "lat"), P(None, "lon", "lat"), P("lat"))
    out_specs = P(None, None, "lon", "lat")
    return jax.shard_map(functools.partial(local, n, m), mesh=mesh, in_specs=in_specs, out_specs=out_specs, check_vma=False)
```

time: 128 us -> 20.2 us (0.16)
  local copies, waits for them, and re-layouts: 41.9 us -> 2.46 us
  blocking collectives: 25.9 us -> 0 us
  matrix products: 21.1 us -> 0 us
  Pallas kernels: 0 us -> 17.5 us
  starting transfers between devices: 16.7 us -> 0 us
  waiting for transfers between devices: 16.6 us -> 0 us
  other arithmetic: 5.27 us -> 0 us
    scatter x4 -> x0, local copies, waits for them, and re-layouts: 35.5 us -> none  [tendency(): padded.at[:, :, 1:-1, 0].set(north_rim).at[:, :, 1:-1, -1].set(south_rim)]
    all_gather x3 -> x0, blocking collectives: 25.9 us -> none  [the longest x2 17.9 us: local(): lax.all_gather(ends[None], 'lon', axis=0, tiled=True)]
    dot_general x4 -> x0, matrix products: 21.1 us -> none  [local_level(): jnp.einsum('ikr,fkr->fir', green, weights_level, precision=lax.Precision....]
    pallas_call x0 -> x1, Pallas kernels: none -> 17.5 us  [local(): pl.pallas_call(functools.partial(kernel, n, m), out_shape=jax.ShapeDtypeS...]
    ppermute x10 -> x0, starting transfers between devices: 16.7 us -> none  [the longest x4 10.2 us: padded_2(): lax.ppermute(lax.slice_in_dim(block, 0, width, axis=dim), axis, backward)]
    ppermute x10 -> x0, waiting for transfers between devices: 16.6 us -> none  [the longest x4 11.3 us: padded_2(): lax.ppermute(lax.slice_in_dim(block, block.shape[dim] - width, None, axis...]
    mul x10 -> x0, other arithmetic: 2.74 us -> none  [the longest x2 1.36 us: local(): partial_value = lax.map(local_level, (logs, star * inverse[:, None]))]
    slice x20 -> x0, local copies, waits for them, and re-layouts: 1.67 us -> none  [the longest x6 1.07 us: tendency(): poles = jnp.stack((field[..., 0], field[..., -1]), 0)]
  transfers between devices with their start and end apart: 10 -> 0, of which waited for: 5 -> 0; matrix products, arithmetic and copies ran while one was open for 2% -> 0% of each run, Pallas kernels for 0% -> 0%
where the time goes in v1:
time: 20.2 us; the launch traced here: 20 us
  Pallas kernels  17.5 us (87%)
  local copies, waits for them, and re-layouts  2.46 us (12%)
    pallas_call x1, Pallas kernels, local(): pl.pallas_call(functools.partial(kernel, n, m), out_shape=jax.ShapeDtypeS...  17.5 us
    unnamed x4, local copies, waits for them, and re-layouts  1.75 us
    reshape x1, local copies, waits for them, and re-layouts, local(): return out.transpose(1, 0, 2).reshape(state.shape)  0.71 us

profile of v1, /device:TPU:0, one launch (start us, length us, event | category | flops | bytes accessed | tf_op | source)
XLA Modules:
  0.0 20.0 jit_solution(13972709125200585195)
XLA Ops:
  0.0 0.8 %copy.5.c_ref = f32[2,45,128]{2,1,0:T(8,128)S(1)} copy(f32[2,45,128]{2,0,1:T(2,128)} %param.4) | data formatting | bytes 92160 | tf_op args[1]
  0.8 0.0 copy-start
  0.8 1.0 %copy.4.x_ref = f32[2,4,45,128]{3,2,1,0:T(8,128)S(1)} copy(f32[2,4,45,128]{3,1,2,0:T(4,128)} %param.3) | data formatting | bytes 368640 | tf_op args[0]
  1.8 0.0 copy-done
  1.8 17.5 %shard_map.37 = f32[45,8,128]{2,1,0:T(8,128)S(1)} custom-call(f32[2,4,45,128]{3,2,1,0:T(8,128)S(1)} %copy.4.x_ref, f32[2,45,128]{2,1,0:T(8,128)S(1)} %copy.5.c_ref, s32[1,128]{1,0:T(1,128)S(1)} %bitcast.5), custom_call_target="tpu_custom_call" | custom-call | tf_op jit(solution)/shard_map/pallas_call | solution.py:183
  19.3 0.7 %copy.6 = f32[2,4,45,128]{3,1,2,0:T(4,128)} copy(f32[2,4,45,128]{3,1,0,2:T(4,128)S(1)} %bitcast.4) | data formatting | bytes 368640 | tf_op jit(solution)/shard_map/reshape | solution.py:210
Async XLA Ops:
  0.8 1.0 %copy-start = (s32[128]{0:T(128)S(1)}, s32[128]{0:T(128)}, u32[]{:S(2)}) copy-start(s32[128]{0:T(128)} %param.5) | copy-start | bytes 1540

commit v2 on v1

v2 whole, which is shorter than its diff:
```python
import functools

import jax
import jax.numpy as jnp
from jax import lax
from jax.experimental import pallas as pl
from jax.experimental.pallas import tpu as pltpu
from jax.sharding import PartitionSpec as P

ITERS = 2
MESH = pl.DeviceIdType.MESH


def kernel(n, m, x_hbm, c_hbm, mask_hbm, out_ref, x_in, c_in, mask_ref, X, inv8, carried, part, fed, edge, mid,
           lonh, lats, lath, gains, ends, own,
           in_sem, lon_send, lon_recv, lat_send, lat_recv, all_send, all_recv):
    levels, L, comps, R = x_in.shape
    S = levels * comps
    lon = lax.axis_index("lon")
    lat = lax.axis_index("lat")
    east = lax.rem(lon + 1, n)
    west = lax.rem(lon + n - 1, n)
    across = lax.rem(lon + n // 2, n)
    first = lat == 0
    last = lat == m - 1
    north = (jnp.where(first, across, lon), jnp.where(first, lat, lat - 1))
    south = (jnp.where(last, across, lon), jnp.where(last, lat, lat + 1))
    north_slot = jnp.where(first, 0, 1)
    south_slot = jnp.where(last, 1, 0)

    def over_ring(step):
        if n <= 16:
            for k in range(1, n):
                step(k)
        else:
            lax.fori_loop(1, n, lambda k, _: (step(k), 0)[1], 0)

    barrier = pltpu.get_barrier_semaphore()
    x_copy = pltpu.make_async_copy(x_hbm, x_in, in_sem.at[0])
    c_copy = pltpu.make_async_copy(c_hbm, c_in, in_sem.at[1])
    mask_copy = pltpu.make_async_copy(mask_hbm, mask_ref, in_sem.at[2])
    x_copy.start()
    c_copy.start()
    mask_copy.start()
    pl.semaphore_signal(barrier, inc=1, device_id=north, device_id_type=MESH)
    pl.semaphore_signal(barrier, inc=1, device_id=south, device_id_type=MESH)
    over_ring(lambda k: pl.semaphore_signal(
        barrier, inc=1, device_id=(lax.rem(lon + k, n), lat), device_id_type=MESH))

    sub = lax.broadcasted_iota(jnp.int32, (S, R), 0)
    lane = lax.broadcasted_iota(jnp.int32, (S, R), 1)
    comp = sub % comps
    lower = sub < comps
    is_north = lane == 0
    is_south = lane == R - 1
    even = lane % 2 == 0
    pair = ((lane + 1) % R) // 2

    def by_level(rows):
        return jnp.where(lower, jnp.broadcast_to(rows[0], (S, R)), jnp.broadcast_to(rows[1], (S, R)))

    row_ids = (lat * R + lane).astype(jnp.float32)
    turning = 0.5 * jnp.sin(jnp.pi / 2 - (row_ids + 0.5) * (jnp.pi / (R * m)))
    turn_u = jnp.where(comp == 0, turning, 0.0)
    turn_v = jnp.where(comp == 1, -turning, 0.0)
    flips = jnp.where(comp < 2, -1.0, 1.0)

    def pack(values, it):
        rim = values(0)
        for i in range(1, L):
            rim = jnp.where(pair == i, pltpu.roll(values(i), 2 * i, 1), rim)
        lats[it] = rim

    def halo_copies(src, it):
        return [
            pltpu.make_async_remote_copy(
                src_ref=lats.at[it], dst_ref=lath.at[it, north_slot], send_sem=lat_send.at[it, 0],
                recv_sem=lat_recv.at[it, north_slot], device_id=north, device_id_type=MESH),
            pltpu.make_async_remote_copy(
                src_ref=lats.at[it], dst_ref=lath.at[it, south_slot], send_sem=lat_send.at[it, 1],
                recv_sem=lat_recv.at[it, south_slot], device_id=south, device_id_type=MESH),
            pltpu.make_async_remote_copy(
                src_ref=src.at[L - 1], dst_ref=lonh.at[it, 0], send_sem=lon_send.at[it, 0],
                recv_sem=lon_recv.at[it, 0], device_id=(east, lat), device_id_type=MESH),
            pltpu.make_async_remote_copy(
                src_ref=src.at[0], dst_ref=lonh.at[it, 1], send_sem=lon_send.at[it, 1],
                recv_sem=lon_recv.at[it, 1], device_id=(west, lat), device_id_type=MESH),
        ]

    def gather_start(src, dst, sem):
        over_ring(lambda k: pltpu.make_async_remote_copy(
            src_ref=src, dst_ref=dst.at[k - 1], send_sem=all_send.at[sem],
            recv_sem=all_recv.at[sem], device_id=(lax.rem(lon + n - k, n), lat),
            device_id_type=MESH).start())

    def wait_for(ref, sem):
        pltpu.make_async_copy(ref, ref, sem).wait()

    def fold(step, start):
        if n <= 16:
            for k in range(n - 1):
                start = step(k, start)
            return start
        return lax.fori_loop(0, n - 1, step, start)

    x_copy.wait()
    for i in range(L):
        X[i] = jnp.concatenate([x_in[l, i] for l in range(levels)], axis=0)
    pack(lambda i: X[i], 0)
    pl.semaphore_wait(barrier, n + 1)
    halos = halo_copies(X, 0)
    for copy in halos:
        copy.start()

    c_copy.wait()
    mask_copy.wait()
    band = mask_ref[...] == 1
    for i in range(L):
        inv = jnp.where(band, 1.0 / (1.0 + c_in[i]), 1.0)
        inv8[i] = by_level([inv[l:l + 1] for l in range(levels)])
    gain = 1.0 - inv8[0]
    carried[0] = gain
    for i in range(1, L):
        gain = gain * (1.0 - inv8[i])
        carried[i] = gain
    gather_start(carried.at[L - 1], gains, 0)

    ring = None
    for it in range(ITERS):
        src = X if it == 0 else mid
        for i in range(L):
            x = src[i]
            no = jnp.where(is_north, 0.0, pltpu.roll(x, 1, 1))
            so = jnp.where(is_south, 0.0, pltpu.roll(x, R - 1, 1))
            u = by_level([src[i, l * comps:l * comps + 1, :] for l in range(levels)])
            v = by_level([src[i, l * comps + 1:l * comps + 2, :] for l in range(levels)])
            if i == 0:
                sides = src[1]
            elif i == L - 1:
                sides = src[L - 2]
            else:
                sides = src[i + 1] + src[i - 1]
            quarter = 0.25 * v
            star = X[i] + (0.1 * (sides + no + so) - 0.4 * x) - quarter * (no - so) + (turn_u * v + turn_v * u)
            inv = inv8[i]
            fed[i] = star * inv
            edge[i] = inv * jnp.where(is_north, 0.1 - quarter, jnp.where(is_south, 0.1 + quarter, 0.0))
        wait_for(lath.at[it, 0], lat_recv.at[it, 0])
        wait_for(lath.at[it, 1], lat_recv.at[it, 1])
        rim_n = lath[it, 0]
        rim_n = jnp.where(first, rim_n * flips, pltpu.roll(rim_n, 1, 1))
        rim_s = lath[it, 1]
        rim_s = jnp.where(last, rim_s * flips, pltpu.roll(rim_s, R - 1, 1))
        rim = jnp.where(even, rim_n, rim_s)
        halos[2].wait_recv()
        halos[3].wait_recv()
        value = None
        for i in range(L):
            inv = inv8[i]
            feed = fed[i] + edge[i] * (pltpu.roll(rim, (R - 2 * i) % R, 1) if i else rim)
            if i == 0:
                feed = feed + (0.1 * inv) * lonh[it, 0]
            if i == L - 1:
                feed = feed + (0.1 * inv) * lonh[it, 1]
            value = feed if i == 0 else (1.0 - inv) * value + feed
            part[i] = value
        own[it] = value
        gather_start(own.at[it], ends.at[it], 1 + it)
        if it == 0:
            wait_for(gains, all_recv.at[0])
            ring = 1.0 / (1.0 - fold(lambda k, t: t * gains[k], carried[L - 1]))
        wait_for(ends.at[it], all_recv.at[1 + it])
        inflow = fold(lambda k, r: r * gains[k] + ends[it, k], value) * ring
        if it + 1 < ITERS:
            for i in range(L):
                mid[i] = 0.5 * (X[i] + (part[i] + carried[i] * inflow))
            pack(lambda i: mid[i], it + 1)
            for copy in halos:
                copy.wait_send()
            halos = halo_copies(mid, it + 1)
            for copy in halos:
                copy.start()
        else:
            for i in range(L):
                result = part[i] + carried[i] * inflow
                for l in range(levels):
                    out_ref[l, i] = result[l * comps:(l + 1) * comps]
    for copy in halos:
        copy.wait_send()
    for sem in range(1 + ITERS):
        wait_for(gains, all_send.at[sem])


def local(n, m, state, courant, band_mask):
    levels, comps, L, R = state.shape
    S = levels * comps
    f32 = jnp.float32
    cell = pltpu.VMEM((L, S, R), f32)
    out = pl.pallas_call(
        functools.partial(kernel, n, m),
        out_shape=jax.ShapeDtypeStruct((levels, L, comps, R), f32),
        in_specs=[
            pl.BlockSpec(memory_space=pltpu.HBM),
            pl.BlockSpec(memory_space=pltpu.HBM),
            pl.BlockSpec(memory_space=pltpu.HBM),
        ],
        out_specs=pl.BlockSpec(memory_space=pltpu.VMEM),
        scratch_shapes=[
            pltpu.VMEM((levels, L, comps, R), f32),
            pltpu.VMEM((L, levels, R), f32),
            pltpu.VMEM((1, R), jnp.int32),
            cell, cell, cell, cell, cell, cell, cell,
            pltpu.VMEM((ITERS, 2, S, R), f32),
            pltpu.VMEM((ITERS, S, R), f32),
            pltpu.VMEM((ITERS, 2, S, R), f32),
            pltpu.VMEM((n - 1, S, R), f32),
            pltpu.VMEM((ITERS, n - 1, S, R), f32),
            pltpu.VMEM((ITERS, S, R), f32),
            pltpu.SemaphoreType.DMA((3,)),
            pltpu.SemaphoreType.DMA((ITERS, 2)),
            pltpu.SemaphoreType.DMA((ITERS, 2)),
            pltpu.SemaphoreType.DMA((ITERS, 2)),
            pltpu.SemaphoreType.DMA((ITERS, 2)),
            pltpu.SemaphoreType.DMA((1 + ITERS,)),
            pltpu.SemaphoreType.DMA((1 + ITERS,)),
        ],
        compiler_params=pltpu.CompilerParams(
            collective_id=0, has_side_effects=True, vmem_limit_bytes=64 * 2**20 - 2**17),
    )(state.transpose(0, 2, 1, 3), courant.transpose(1, 0, 2), band_mask.reshape(1, R))
    return out.transpose(0, 2, 1, 3)


def solution(mesh):
    n, m = mesh.shape["lon"], mesh.shape["lat"]
    in_specs = (P(None, None, "lon", "lat"), P(None, "lon", "lat"), P("lat"))
    out_specs = P(None, None, "lon", "lat")
    return jax.shard_map(functools.partial(local, n, m), mesh=mesh, in_specs=in_specs, out_specs=out_specs, check_vma=False)
```

time: 20.2 us -> 19.8 us (0.980)
  local copies, waits for them, and re-layouts: 2.46 us -> 1.61 us
  Pallas kernels: 17.5 us -> 18 us
    reshape x1 -> x0, local copies, waits for them, and re-layouts: 0.71 us -> none  [local(): return out.transpose(1, 0, 2).reshape(state.shape)]
    pallas_call x1, Pallas kernels: 17.5 us -> 18 us  [local(): pl.pallas_call(functools.partial(kernel, n, m), out_shape=jax.ShapeDtypeS...]
    unnamed x4 -> x1, local copies, waits for them, and re-layouts: 1.75 us -> 1.61 us
where the time goes in v2:
time: 19.8 us; the launch traced here: 19.6 us
  Pallas kernels  18 us (91%)
  local copies, waits for them, and re-layouts  1.61 us (8%)
    pallas_call x1, Pallas kernels, local(): pl.pallas_call(functools.partial(kernel, n, m), out_shape=jax.ShapeDtypeS...  18 us
    unnamed x1, local copies, waits for them, and re-layouts  1.61 us

profile of v2, /device:TPU:0, one launch (start us, length us, event | category | flops | bytes accessed | tf_op | source)
XLA Modules:
  0.0 19.6 jit_solution(14830453947036877811)
XLA Ops:
  0.0 18.0 %shard_map.37 = f32[2,45,4,128]{3,2,1,0:T(4,128)} custom-call(f32[2,45,4,128]{3,2,1,0:T(4,128)} %bitcast.5, f32[45,2,128]{2,1,0:T(2,128)} %bitcast.6, s32[1,128]{1,0:T(1,128)} %bitcast.7), custom_call_target="tpu_custom_call" | custom-call | tf_op jit(solution)/shard_map/pallas_call | solution.py:199
  18.0 1.6 %copy.5 = f32[2,4,45,128]{3,1,2,0:T(4,128)} copy(f32[2,4,45,128]{3,1,2,0:T(4,128)} %bitcast.4) | data formatting | bytes 368640

commit v3 on v2

v3 whole, which is shorter than its diff:
```python
import functools

import jax
import jax.numpy as jnp
from jax import lax
from jax.experimental import pallas as pl
from jax.experimental.pallas import tpu as pltpu
from jax.sharding import PartitionSpec as P

MESH = pl.DeviceIdType.MESH


def kernel(n, m, x_hbm, c_hbm, mask_hbm, out_ref, x_in, c_in, mask_ref, X, inv8, carried, part, fed, edge, mid,
           side_inv, side_x, side_part, side_carried, rows,
           rim_out, rim_in, ring_out, ring_in, ends_out, ends_in, last_out, last_in,
           in_sem, send_sem, recv_sem):
    levels, L, comps, R = x_in.shape
    S = levels * comps
    lon = lax.axis_index("lon")
    lat = lax.axis_index("lat")
    first = lat == 0
    last = lat == m - 1
    north_lat = jnp.where(first, lat, lat - 1)
    south_lat = jnp.where(last, lat, lat + 1)
    north_shift = jnp.where(first, n // 2, 0)
    south_shift = jnp.where(last, n // 2, 0)
    north_slot = jnp.where(first, 0, 1)
    south_slot = jnp.where(last, 1, 0)

    def shifted(k):
        return lax.rem(lon + (k + n), n)

    rim_peers = [
        (shifted(shift + e), to_lat, slot, e)
        for e in (0, 1, -1)
        for shift, to_lat, slot in ((north_shift, north_lat, north_slot), (south_shift, south_lat, south_slot))
    ]

    def over_middle(step, low, high):
        if n <= 16:
            for k in range(low, high):
                step(k)
        else:
            lax.fori_loop(low, high, lambda k, _: (step(k), 0)[1], 0)

    barrier = pltpu.get_barrier_semaphore()
    x_copy = pltpu.make_async_copy(x_hbm, x_in, in_sem.at[0])
    c_copy = pltpu.make_async_copy(c_hbm, c_in, in_sem.at[1])
    mask_copy = pltpu.make_async_copy(mask_hbm, mask_ref, in_sem.at[2])
    x_copy.start()
    c_copy.start()
    mask_copy.start()
    for to_lon, to_lat, _, _ in rim_peers:
        pl.semaphore_signal(barrier, inc=1, device_id=(to_lon, to_lat), device_id_type=MESH)
    over_middle(lambda k: pl.semaphore_signal(
        barrier, inc=1, device_id=(shifted(k), lat), device_id_type=MESH), 1, n)

    sub = lax.broadcasted_iota(jnp.int32, (S, R), 0)
    lane = lax.broadcasted_iota(jnp.int32, (S, R), 1)
    comp = sub % comps
    lower = sub < comps
    is_north = lane == 0
    is_south = lane == R - 1
    even = lane % 2 == 0
    pair = ((lane + 1) % R) // 2
    second_pair = jnp.where(even, ((lane + 2) % R) // 2, lane // 2)

    def roll(value, shift):
        shift = shift % R
        return pltpu.roll(value, shift, 1) if shift else value

    def by_level(values):
        return jnp.where(lower, jnp.broadcast_to(values[0], (S, R)), jnp.broadcast_to(values[1], (S, R)))

    def winds(ref, i):
        u = by_level([ref[i, l * comps:l * comps + 1, :] for l in range(levels)])
        v = by_level([ref[i, l * comps + 1:l * comps + 2, :] for l in range(levels)])
        return u, v

    def turns(row_ids):
        turning = 0.5 * jnp.sin(jnp.pi / 2 - (row_ids.astype(jnp.float32) + 0.5) * (jnp.pi / (R * m)))
        return jnp.where(comp == 0, turning, 0.0), jnp.where(comp == 1, -turning, 0.0)

    turn_u, turn_v = turns(lat * R + lane)
    side_turn_u, side_turn_v = turns(jnp.where(
        even, jnp.where(first, 0, lat * R - 1), jnp.where(last, R * m - 1, lat * R + R)))
    flips = jnp.where(comp < 2, -1.0, 1.0)

    def remote(src, dst, sem, device):
        return pltpu.make_async_remote_copy(
            src_ref=src, dst_ref=dst, send_sem=send_sem.at[sem], recv_sem=recv_sem.at[sem],
            device_id=device, device_id_type=MESH)

    def wait_for(ref, sem):
        pltpu.make_async_copy(ref, ref, sem).wait()

    def fold(step, start, low, high):
        if n <= 16:
            for k in range(low, high):
                start = step(k, start)
            return start
        return lax.fori_loop(low, high, step, start)

    x_copy.wait()
    for i in range(L):
        value = jnp.concatenate([x_in[l, i] for l in range(levels)], axis=0)
        X[i] = value
        moved = roll(value, 2 * i)
        rim0 = moved if i == 0 else jnp.where(pair == i, moved, rim0)
        rim1 = moved if i == 0 else jnp.where(second_pair == i, moved, rim1)
    rim_out[0] = rim0
    rim_out[2] = rim1
    c_copy.wait()
    mask_copy.wait()
    band = mask_ref[...] == 1
    for i in range(L):
        inv = jnp.where(band, 1.0 / (1.0 + c_in[i]), 1.0)
        inv = by_level([inv[l:l + 1] for l in range(levels)])
        inv8[i] = inv
        moved = roll(inv, 2 * i)
        rim2 = moved if i == 0 else jnp.where(pair == i, moved, rim2)
    rim_out[1] = rim2

    pl.semaphore_wait(barrier, n - 1 + 6)
    for to_lon, to_lat, slot, e in rim_peers:
        if e == 0:
            remote(rim_out, rim_in.at[pl.ds(3 * slot, 3)], 0, (to_lon, to_lat)).start()
        else:
            corner = 6 + 2 * slot + (0 if e == 1 else 1)
            remote(rim_out.at[pl.ds(0, 1)], rim_in.at[pl.ds(corner, 1)], 0, (to_lon, to_lat)).start()
    gain = 1.0 - inv8[0]
    carried[0] = gain
    ring_out[2] = gain
    for i in range(1, L):
        gain = gain * (1.0 - inv8[i])
        carried[i] = gain
    ring_out[0] = X[L - 1]
    ring_out[1] = gain
    ring_out[3] = X[0]
    remote(ring_out.at[pl.ds(0, 2)], ring_in.at[pl.ds(n, 2)], 1, (shifted(1), lat)).start()
    remote(ring_out.at[pl.ds(1, 3)], ring_in.at[pl.ds(0, 3)], 1, (shifted(-1), lat)).start()
    over_middle(lambda k: remote(
        ring_out.at[pl.ds(1, 1)], ring_in.at[pl.ds(k + 1, 1)], 1, (shifted(-k), lat)).start(), 2, n - 1)

    for i in range(L):
        x = X[i]
        no = jnp.where(is_north, 0.0, roll(x, 1))
        so = jnp.where(is_south, 0.0, roll(x, -1))
        u, v = winds(X, i)
        if i == 0:
            sides = X[1]
        elif i == L - 1:
            sides = X[L - 2]
        else:
            sides = X[i + 1] + X[i - 1]
        quarter = 0.25 * v
        star = x + (0.1 * (sides + no + so) - 0.4 * x) - quarter * (no - so) + (turn_u * v + turn_v * u)
        inv = inv8[i]
        fed[i] = star * inv
        edge[i] = inv * jnp.where(is_north, 0.1 - quarter, jnp.where(is_south, 0.1 + quarter, 0.0))

    wait_for(rim_in, recv_sem.at[0])

    def beside(from_north, from_south, flip):
        a = jnp.where(first, from_north * flip, roll(from_north, 1))
        b = jnp.where(last, from_south * flip, roll(from_south, -1))
        return jnp.where(even, a, b)

    center = beside(rim_in[0], rim_in[3], flips)
    packed_inv = beside(rim_in[1], rim_in[4], 1.0)
    for i in range(L):
        side_x[i] = roll(center, -2 * i)
        side_inv[i] = roll(packed_inv, -2 * i)
    outer_n = jnp.where(first, roll(rim_in[2], -1) * flips, roll(rim_in[2], 2))
    outer_s = jnp.where(last, roll(rim_in[5], 1) * flips, roll(rim_in[5], -2))
    outer = jnp.where(even, outer_n, outer_s)
    inner = rim_out[0]
    corner_w = beside(rim_in[6], rim_in[8], flips)
    corner_e = beside(rim_in[7], rim_in[9], flips)
    east = jnp.where(pair == L - 1, roll(corner_e, 2 * L - 2), roll(center, -2))
    west = jnp.where(pair == 0, roll(corner_w, 2 - 2 * L), roll(center, 2))
    no = jnp.where(even, outer, inner)
    so = jnp.where(even, inner, outer)
    rows[0] = center
    u, v = winds(rows, 0)
    star = center + (0.1 * (east + west + no + so) - 0.4 * center) - (0.25 * v) * (no - so)
    star = star + (side_turn_u * v + side_turn_v * u)
    packed_feed = star * packed_inv

    wait_for(ring_in, recv_sem.at[1])
    for i in range(L):
        rate = 1.0 - inv8[i]
        feed = fed[i] + edge[i] * side_x[i]
        if i == 0:
            feed = feed + (0.1 * inv8[i]) * ring_in[n]
        if i == L - 1:
            feed = feed + (0.1 * inv8[i]) * ring_in[2]
        side_rate = 1.0 - side_inv[i]
        side_feed = roll(packed_feed, -2 * i)
        if i == 0:
            value, side_value, side_gain = feed, side_feed, side_rate
            ends_out[0] = feed
        else:
            value = rate * value + feed
            side_value = side_rate * side_value + side_feed
            side_gain = side_gain * side_rate
        part[i] = value
        side_part[i] = side_value
        side_carried[i] = side_gain
    ends_out[1] = value
    ends_out[2] = side_value
    ends_out[3] = side_gain
    over_middle(lambda k: remote(
        ends_out.at[pl.ds(1, 3)], ends_in.at[pl.ds(3 * k - 2, 3)], 2, (shifted(-k), lat)).start(), 2, n)
    remote(ends_out, ends_in.at[pl.ds(0, 4)], 2, (shifted(-1), lat)).start()

    def gain_of(k):
        return ring_in[k + 1]

    total = gain * ring_in[0]
    total = fold(lambda k, t: t * gain_of(k), total, 2, n - 1) * ring_in[n + 1]
    ring = 1.0 / (1.0 - total)

    wait_for(ends_in, recv_sem.at[2])
    run = value * ring_in[0] + ends_in[1]
    run = fold(lambda k, r: r * gain_of(k) + ends_in[3 * k - 2], run, 2, n - 1)
    inflow = (run * ring_in[n + 1] + ends_in[3 * n - 5]) * ring

    def side_step(k, both):
        run, total = both
        return run * ends_in[3 * k] + ends_in[3 * k - 1], total * ends_in[3 * k]

    side_run, side_total = fold(side_step, (side_value, side_gain), 1, n)
    side_inflow = side_run / (1.0 - side_total)

    last_cell = value + gain * inflow
    mid_w = 0.5 * (ring_in[n] + inflow)
    mid_e = 0.5 * (ring_in[2] + (ends_in[0] + ring_in[1] * last_cell))
    for i in range(L):
        mid[i] = 0.5 * (X[i] + (part[i] + carried[i] * inflow))
    for i in range(L):
        x = mid[i]
        beyond = 0.5 * (side_x[i] + (side_part[i] + side_carried[i] * side_inflow))
        no = jnp.where(is_north, beyond, roll(x, 1))
        so = jnp.where(is_south, beyond, roll(x, -1))
        e = mid[i + 1] if i + 1 < L else mid_e
        w = mid[i - 1] if i > 0 else mid_w
        u, v = winds(mid, i)
        star = X[i] + (0.1 * (e + w + no + so) - 0.4 * x) - (0.25 * v) * (no - so) + (turn_u * v + turn_v * u)
        inv = inv8[i]
        feed = star * inv
        value = feed if i == 0 else (1.0 - inv) * value + feed
        part[i] = value
    last_out[...] = value
    over_middle(lambda k: remote(
        last_out, last_in.at[k - 1], 3, (shifted(-k), lat)).start(), 1, n)
    wait_for(last_in, recv_sem.at[3])
    run = value * ring_in[0] + last_in[0]
    run = fold(lambda k, r: r * gain_of(k) + last_in[k - 1], run, 2, n - 1)
    inflow = (run * ring_in[n + 1] + last_in[n - 2]) * ring
    for i in range(L):
        result = part[i] + carried[i] * inflow
        for l in range(levels):
            out_ref[l, i] = result[l * comps:(l + 1) * comps]
    for sem, ref in enumerate((rim_in, ring_in, ends_in, last_in)):
        wait_for(ref, send_sem.at[sem])


def local(n, m, state, courant, band_mask):
    levels, comps, L, R = state.shape
    S = levels * comps
    f32 = jnp.float32

    def cells(count):
        return pltpu.VMEM((count, S, R), f32)

    out = pl.pallas_call(
        functools.partial(kernel, n, m),
        out_shape=jax.ShapeDtypeStruct((levels, L, comps, R), f32),
        in_specs=[pl.BlockSpec(memory_space=pltpu.HBM)] * 3,
        out_specs=pl.BlockSpec(memory_space=pltpu.VMEM),
        scratch_shapes=[
            pltpu.VMEM((levels, L, comps, R), f32),
            pltpu.VMEM((L, levels, R), f32),
            pltpu.VMEM((1, R), jnp.int32),
            *[cells(L)] * 11,
            cells(1),
            cells(3),
            cells(10),
            cells(4),
            cells(n + 2),
            cells(4),
            cells(3 * n - 2),
            pltpu.VMEM((S, R), f32),
            cells(n - 1),
            pltpu.SemaphoreType.DMA((3,)),
            pltpu.SemaphoreType.DMA((4,)),
            pltpu.SemaphoreType.DMA((4,)),
        ],
        compiler_params=pltpu.CompilerParams(
            collective_id=0, has_side_effects=True, vmem_limit_bytes=64 * 2**20 - 2**17),
    )(state.transpose(0, 2, 1, 3), courant.transpose(1, 0, 2), band_mask.reshape(1, R))
    return out.transpose(0, 2, 1, 3)


def solution(mesh):
    n, m = mesh.shape["lon"], mesh.shape["lat"]
    in_specs = (P(None, None, "lon", "lat"), P(None, "lon", "lat"), P("lat"))
    out_specs = P(None, None, "lon", "lat")
    return jax.shard_map(functools.partial(local, n, m), mesh=mesh, in_specs=in_specs, out_specs=out_specs, check_vma=False)
```

time: 19.8 us -> 17.4 us (0.88)
  Pallas kernels: 18 us -> 15.6 us
    pallas_call x1, Pallas kernels: 18 us -> 15.6 us  [local(): pl.pallas_call(functools.partial(kernel, n, m), out_shape=jax.ShapeDtypeS...]
where the time goes in v3:
time: 17.4 us; the launch traced here: 17.2 us
  Pallas kernels  15.6 us (90%)
  local copies, waits for them, and re-layouts  1.61 us (9%)
    pallas_call x1, Pallas kernels, local(): pl.pallas_call(functools.partial(kernel, n, m), out_shape=jax.ShapeDtypeS...  15.6 us
    unnamed x1, local copies, waits for them, and re-layouts  1.61 us

profile of v3, /device:TPU:0, one launch (start us, length us, event | category | flops | bytes accessed | tf_op | source)
XLA Modules:
  0.0 17.2 jit_solution(2715419393661308243)
XLA Ops:
  0.0 15.6 %shard_map.37 = f32[2,45,4,128]{3,2,1,0:T(4,128)} custom-call(f32[2,45,4,128]{3,2,1,0:T(4,128)} %bitcast.5, f32[45,2,128]{2,1,0:T(2,128)} %bitcast.6, s32[1,128]{1,0:T(1,128)} %bitcast.7), custom_call_target="tpu_custom_call" | custom-call | tf_op jit(solution)/shard_map/pallas_call | solution.py:277
  15.6 1.6 %copy.5 = f32[2,4,45,128]{3,1,2,0:T(4,128)} copy(f32[2,4,45,128]{3,1,2,0:T(4,128)} %bitcast.4) | data formatting | bytes 368640

commit v4 on v3

--- a/solution.py
+++ b/solution.py
@@ -12,7 +12,7 @@
 
 def kernel(n, m, x_hbm, c_hbm, mask_hbm, out_ref, x_in, c_in, mask_ref, X, inv8, carried, part, fed, edge, mid,
            side_inv, side_x, side_part, side_carried, rows,
-           rim_out, rim_in, ring_out, ring_in, ends_out, ends_in, last_out, last_in,
+           rim_out, rim_in, column_in, ring_out, ring_in, ends_out, ends_in, last_out, last_in,
            in_sem, send_sem, recv_sem):
     levels, L, comps, R = x_in.shape
     S = levels * comps
@@ -123,6 +123,9 @@
 
     pl.semaphore_wait(barrier, n - 1 + 6)
     for to_lon, to_lat, slot, e in rim_peers:
+        if e == 1 and slot is north_slot:
+            remote(X.at[pl.ds(L - 1, 1)], column_in.at[pl.ds(0, 1)], 4, (shifted(1), lat)).start()
+            remote(X.at[pl.ds(0, 1)], column_in.at[pl.ds(1, 1)], 4, (shifted(-1), lat)).start()
         if e == 0:
             remote(rim_out, rim_in.at[pl.ds(3 * slot, 3)], 0, (to_lon, to_lat)).start()
         else:
@@ -130,17 +133,14 @@
             remote(rim_out.at[pl.ds(0, 1)], rim_in.at[pl.ds(corner, 1)], 0, (to_lon, to_lat)).start()
     gain = 1.0 - inv8[0]
     carried[0] = gain
-    ring_out[2] = gain
+    ring_out[1] = gain
     for i in range(1, L):
         gain = gain * (1.0 - inv8[i])
         carried[i] = gain
-    ring_out[0] = X[L - 1]
-    ring_out[1] = gain
-    ring_out[3] = X[0]
-    remote(ring_out.at[pl.ds(0, 2)], ring_in.at[pl.ds(n, 2)], 1, (shifted(1), lat)).start()
-    remote(ring_out.at[pl.ds(1, 3)], ring_in.at[pl.ds(0, 3)], 1, (shifted(-1), lat)).start()
+    ring_out[0] = gain
+    remote(ring_out, ring_in.at[pl.ds(0, 2)], 1, (shifted(-1), lat)).start()
     over_middle(lambda k: remote(
-        ring_out.at[pl.ds(1, 1)], ring_in.at[pl.ds(k + 1, 1)], 1, (shifted(-k), lat)).start(), 2, n - 1)
+        ring_out.at[pl.ds(0, 1)], ring_in.at[pl.ds(k, 1)], 1, (shifted(-k), lat)).start(), 2, n)
 
     for i in range(L):
         x = X[i]
@@ -187,14 +187,14 @@
     star = star + (side_turn_u * v + side_turn_v * u)
     packed_feed = star * packed_inv
 
-    wait_for(ring_in, recv_sem.at[1])
+    wait_for(column_in, recv_sem.at[4])
     for i in range(L):
         rate = 1.0 - inv8[i]
         feed = fed[i] + edge[i] * side_x[i]
         if i == 0:
-            feed = feed + (0.1 * inv8[i]) * ring_in[n]
+            feed = feed + (0.1 * inv8[i]) * column_in[0]
         if i == L - 1:
-            feed = feed + (0.1 * inv8[i]) * ring_in[2]
+            feed = feed + (0.1 * inv8[i]) * column_in[1]
         side_rate = 1.0 - side_inv[i]
         side_feed = roll(packed_feed, -2 * i)
         if i == 0:
@@ -215,16 +215,17 @@
     remote(ends_out, ends_in.at[pl.ds(0, 4)], 2, (shifted(-1), lat)).start()
 
     def gain_of(k):
-        return ring_in[k + 1]
-
+        return ring_in[k]
+
+    wait_for(ring_in, recv_sem.at[1])
     total = gain * ring_in[0]
-    total = fold(lambda k, t: t * gain_of(k), total, 2, n - 1) * ring_in[n + 1]
+    total = fold(lambda k, t: t * gain_of(k), total, 2, n - 1) * ring_in[n - 1]
     ring = 1.0 / (1.0 - total)
 
     wait_for(ends_in, recv_sem.at[2])
     run = value * ring_in[0] + ends_in[1]
     run = fold(lambda k, r: r * gain_of(k) + ends_in[3 * k - 2], run, 2, n - 1)
-    inflow = (run * ring_in[n + 1] + ends_in[3 * n - 5]) * ring
+    inflow = (run * ring_in[n - 1] + ends_in[3 * n - 5]) * ring
 
     def side_step(k, both):
         run, total = both
@@ -234,8 +235,8 @@
     side_inflow = side_run / (1.0 - side_total)
 
     last_cell = value + gain * inflow
-    mid_w = 0.5 * (ring_in[n] + inflow)
-    mid_e = 0.5 * (ring_in[2] + (ends_in[0] + ring_in[1] * last_cell))
+    mid_w = 0.5 * (column_in[0] + inflow)
+    mid_e = 0.5 * (column_in[1] + (ends_in[0] + ring_in[1] * last_cell))
     for i in range(L):
         mid[i] = 0.5 * (X[i] + (part[i] + carried[i] * inflow))
     for i in range(L):
@@ -257,12 +258,12 @@
     wait_for(last_in, recv_sem.at[3])
     run = value * ring_in[0] + last_in[0]
     run = fold(lambda k, r: r * gain_of(k) + last_in[k - 1], run, 2, n - 1)
-    inflow = (run * ring_in[n + 1] + last_in[n - 2]) * ring
+    inflow = (run * ring_in[n - 1] + last_in[n - 2]) * ring
     for i in range(L):
         result = part[i] + carried[i] * inflow
         for l in range(levels):
             out_ref[l, i] = result[l * comps:(l + 1) * comps]
-    for sem, ref in enumerate((rim_in, ring_in, ends_in, last_in)):
+    for sem, ref in enumerate((rim_in, ring_in, ends_in, last_in, column_in)):
         wait_for(ref, send_sem.at[sem])
 
 
@@ -287,19 +288,23 @@
             cells(1),
             cells(3),
             cells(10),
-            cells(4),
-            cells(n + 2),
+            cells(2),
+            cells(2),
+            cells(n),
             cells(4),
             cells(3 * n - 2),
             pltpu.VMEM((S, R), f32),
             cells(n - 1),
             pltpu.SemaphoreType.DMA((3,)),
-            pltpu.SemaphoreType.DMA((4,)),
-            pltpu.SemaphoreType.DMA((4,)),
+            pltpu.SemaphoreType.DMA((5,)),
+            pltpu.SemaphoreType.DMA((5,)),
         ],
         compiler_params=pltpu.CompilerParams(
-            collective_id=0, has_side_effects=True, vmem_limit_bytes=64 * 2**20 - 2**17),
-    )(state.transpose(0, 2, 1, 3), courant.transpose(1, 0, 2), band_mask.reshape(1, R))
+            collective_id=0, has_side_effects=True, vmem_limit_bytes=16 * 2**20),
+    )(*[
+        pltpu.with_memory_space_constraint(value, pltpu.HBM)
+        for value in (state.transpose(0, 2, 1, 3), courant.transpose(1, 0, 2), band_mask.reshape(1, R))
+    ])
     return out.transpose(0, 2, 1, 3)
 
 

time: 17.4 us -> 15.8 us (0.908)
  local copies, waits for them, and re-layouts: 1.61 us -> 0.68 us
  Pallas kernels: 15.6 us -> 15 us
    unnamed x1, local copies, waits for them, and re-layouts: 1.61 us -> 0.68 us
    pallas_call x1, Pallas kernels: 15.6 us -> 15 us  [local(): pl.pallas_call(functools.partial(kernel, n, m), out_shape=jax.ShapeDtypeS...]
where the time goes in v4:
time: 15.8 us; the launch traced here: 15.6 us
  Pallas kernels  15 us (95%)
  local copies, waits for them, and re-layouts  0.68 us (4%)
    pallas_call x1, Pallas kernels, local(): pl.pallas_call(functools.partial(kernel, n, m), out_shape=jax.ShapeDtypeS...  15 us
    unnamed x1, local copies, waits for them, and re-layouts  0.68 us

profile of v4, /device:TPU:0, one launch (start us, length us, event | category | flops | bytes accessed | tf_op | source)
XLA Modules:
  0.0 15.6 jit_solution(3747926755646302096)
XLA Ops:
  0.0 15.0 %shard_map.37 = f32[2,45,4,128]{3,2,1,0:T(4,128)S(1)} custom-call(f32[2,45,4,128]{3,2,1,0:T(4,128)} %bitcast.5, f32[45,2,128]{2,1,0:T(2,128)} %bitcast.6, s32[1,128]{1,0:T(1,128)} %bitcast.7), custom_call_target="tpu_custom_call" | custom-call | tf_op jit(solution)/shard_map/pallas_call | solution.py:278
  15.0 0.7 %copy.5 = f32[2,4,45,128]{3,1,2,0:T(4,128)} copy(f32[2,4,45,128]{3,1,2,0:T(4,128)S(1)} %bitcast.4) | data formatting | bytes 368640

commit v5 on v4

--- a/solution.py
+++ b/solution.py
@@ -48,13 +48,13 @@
     c_copy = pltpu.make_async_copy(c_hbm, c_in, in_sem.at[1])
     mask_copy = pltpu.make_async_copy(mask_hbm, mask_ref, in_sem.at[2])
     x_copy.start()
-    c_copy.start()
-    mask_copy.start()
     for to_lon, to_lat, _, _ in rim_peers:
         pl.semaphore_signal(barrier, inc=1, device_id=(to_lon, to_lat), device_id_type=MESH)
     over_middle(lambda k: pl.semaphore_signal(
         barrier, inc=1, device_id=(shifted(k), lat), device_id_type=MESH), 1, n)
 
+    c_copy.start()
+    mask_copy.start()
     sub = lax.broadcasted_iota(jnp.int32, (S, R), 0)
     lane = lax.broadcasted_iota(jnp.int32, (S, R), 1)
     comp = sub % comps
@@ -254,7 +254,8 @@
         part[i] = value
     last_out[...] = value
     over_middle(lambda k: remote(
-        last_out, last_in.at[k - 1], 3, (shifted(-k), lat)).start(), 1, n)
+        last_out, last_in.at[k - 1], 3, (shifted(-k), lat)).start(), 2, n)
+    remote(last_out, last_in.at[0], 3, (shifted(-1), lat)).start()
     wait_for(last_in, recv_sem.at[3])
     run = value * ring_in[0] + last_in[0]
     run = fold(lambda k, r: r * gain_of(k) + last_in[k - 1], run, 2, n - 1)

time: 15.8 us -> 15.7 us (level)
  no operation moved by 1% of the time
where the time goes in v5:
time: 15.7 us; the launch traced here: 15.6 us
  Pallas kernels  14.9 us (95%)
  local copies, waits for them, and re-layouts  0.68 us (4%)
    pallas_call x1, Pallas kernels, local(): pl.pallas_call(functools.partial(kernel, n, m), out_shape=jax.ShapeDtypeS...  14.9 us
    unnamed x1, local copies, waits for them, and re-layouts  0.68 us

profile of v5, /device:TPU:0, one launch (start us, length us, event | category | flops | bytes accessed | tf_op | source)
XLA Modules:
  0.0 15.6 jit_solution(11084233260178521735)
XLA Ops:
  0.0 14.9 %shard_map.37 = f32[2,45,4,128]{3,2,1,0:T(4,128)S(1)} custom-call(f32[2,45,4,128]{3,2,1,0:T(4,128)} %bitcast.5, f32[45,2,128]{2,1,0:T(2,128)} %bitcast.6, s32[1,128]{1,0:T(1,128)} %bitcast.7), custom_call_target="tpu_custom_call" | custom-call | tf_op jit(solution)/shard_map/pallas_call | solution.py:279
  14.9 0.7 %copy.5 = f32[2,4,45,128]{3,1,2,0:T(4,128)} copy(f32[2,4,45,128]{3,1,2,0:T(4,128)S(1)} %bitcast.4) | data formatting | bytes 368640
